TPU v7x, 32 devices: a whole 2x2x4 slice. The times are simulated.
32 devices in a mesh: super: 8 (over z, x), col: 4 (over y, core).
Axes of the slice: x: 2, y: 2, z: 4, core: 2. Of those that a mesh axis runs over, the one named last changes fastest.
Arguments:
- parent: int32 [32, 4], P('super'), may hold values from 0 to 7, as said below
- off_blocks: bfloat16 [32, 4, 512, 512], P('super', None, 'col'), may hold values from -0.25 to 0.25
- inv_factors: bfloat16 [32, 512, 512], P('super', 'col'), as said below
- arrow_rows: bfloat16 [32, 64, 512], P('super'), may hold values from -0.046875 to 0.046875
- target_blocks: float32 [8, 512, 512], P('super'), as said below
- arrow_block: float32 [64, 64], replicated, may hold values from -6 to 6
Outputs:
- factor_blocks: float32 [8, 512, 512], P('super', 'col')
- arrow_update: float32 [64, 64], replicated
Inputs may be any that keep to these rules, and one draw needn't show every extreme that they name: Each eliminated supernode names 4 different parents; among the 16 entries of one index of super at most 2 name the same parent. `inv_factors`: each block is lower triangular. `target_blocks`: each block is symmetric, and stays positive definite after the Schur sums of its children are subtracted.
All inputs are finite; a program needn't handle non-finite values.
Results may differ from a plain program's by a relative error of at most 0.00115.
Values may be sent and summed in bfloat16 or wider, within the bound.
A program may use at most 128 MiB of HBM per device.

v0:
```python
import jax
import jax.numpy as jnp
from jax import lax
from jax.sharding import PartitionSpec as P


def shards(parent, off_blocks, inv_factors, arrow_rows, target_blocks, arrow_block):
    supers = lax.axis_size("super")
    sources = off_blocks.shape[0]
    fanout = off_blocks.shape[1]
    slab_rows = off_blocks.shape[2]
    block_width = off_blocks.shape[3]
    item_count = sources * fanout
    capacity = max(2, (item_count + supers - 1) // supers)
    stacked_rows = off_blocks.reshape(sources, fanout * slab_rows, block_width)
    portion = lax.all_gather(inv_factors, "col", axis=1, tiled=True)
    rows_part = jnp.einsum(
        "jrk,jck->jrc", stacked_rows, portion, preferred_element_type=jnp.float32
    ).astype(jnp.bfloat16)
    arrow_part = jnp.einsum(
        "jak,jck->jac", arrow_rows, portion, preferred_element_type=jnp.float32
    ).astype(jnp.bfloat16)
    formed = jnp.concatenate([rows_part, arrow_part], axis=1)
    row_panels = formed[:, : fanout * slab_rows].reshape(sources, fanout, slab_rows, block_width)
    arrow_panels = formed[:, fanout * slab_rows :]
    arrow_local = jnp.einsum(
        "jac,jbc->ab", arrow_panels, arrow_panels, preferred_element_type=jnp.float32
    )
    arrow_total = lax.psum(arrow_local, "super")
    panels = lax.all_to_all(row_panels, "col", split_axis=3, concat_axis=2, tiled=True)
    column_panels = panels.reshape(item_count, block_width, panels.shape[3])
    owners = parent.reshape(item_count)
    item_index = jnp.arange(item_count, dtype=jnp.int32)
    matching = owners[:, None] == owners[None, :]
    earlier = item_index[None, :] < item_index[:, None]
    position = jnp.sum((matching & earlier).astype(jnp.int32), axis=1)
    target_slot = owners * capacity + position
    slot_match = jnp.arange(supers * capacity, dtype=jnp.int32)[:, None] == target_slot[None, :]
    source_item = jnp.sum(jnp.where(slot_match, item_index[None, :], 0), axis=1)
    filled = jnp.any(slot_match, axis=1)
    packed = jnp.where(
        filled[:, None, None], column_panels[source_item], jnp.zeros((), jnp.bfloat16)
    )
    packed = packed.reshape(supers, capacity, block_width, column_panels.shape[2])
    received = lax.all_to_all(packed, "super", split_axis=0, concat_axis=0, tiled=True)
    partial_terms = jnp.einsum(
        "dmrc,dmsc->mrs", received, received, preferred_element_type=jnp.float32
    )
    schur_local = jnp.sum(partial_terms, axis=0)
    column_index = lax.axis_index("col")
    panel_width = inv_factors.shape[1]
    updated = target_blocks[0] - lax.psum(schur_local.astype(jnp.bfloat16), "col").astype(
        jnp.float32
    )
    factor = jnp.linalg.cholesky(updated)
    factor_rows = lax.dynamic_slice_in_dim(factor, column_index * panel_width, panel_width, 0)
    return (factor_rows[None], arrow_block - arrow_total)


def solution(mesh):
    placed = (
        P("super", None),
        P("super", None, "col", None),
        P("super", "col", None),
        P("super", None, None),
        P("super", None, None),
        P(),
    )
    return jax.shard_map(
        shards,
        mesh=mesh,
        in_specs=placed,
        out_specs=(P("super", "col", None), P()),
        check_vma=False,
    )
```

profile of v0, /device:TPU:0, one launch (start us, length us, event | category | flops | bytes accessed | tf_op | source)
XLA Modules:
  0.0 283.3 jit_solution(7325671771713001273)
XLA Ops:
  7.9 27.0 %all-gather.2.cloned.1.call-done = bf16[4,512,512]{2,1,0:T(8,128)(2,1)} async-done(((bf16[4,128,512]{2,1,0:T(8,128)(2,1)}), bf16[4,512,512]{2,1,0:T(8,128)(2,1)}) %all-gather.2.cloned.1.call-update) | async-done | bytes 2097168 | tf_op jit(solution)/shard_map/all_gather | solution.py:16
  34.9 4.2 %convolution_convert_fusion = bf16[4,512,512]{2,1,0:T(8,128)(2,1)} fusion(bf16[4,512,512]{2,1,0:T(8,128)(2,1)S(1)} %bitcast.49, bf16[4,512,512]{2,1,0:T(8,128)(2,1)} %all-gather.2.cloned.1.call-done), kind=kOutput, calls=%fused_computation.2 | convolution fusion | flops 1074790400 | bytes 6291456 | tf_op jit(solution)/shard_map/jrk,jck->jrc/dot_general | solution.py:17
  39.1 4.5 %copy.26 = bf16[4,4,128,512]{2,1,0,3:T(4,128)(2,1)} copy(bf16[4,4,128,512]{3,2,1,0:T(8,128)(2,1)} %bitcast.53) | data formatting | bytes 4194304 | tf_op jit(solution)/shard_map/reshape | solution.py:24
  43.6 4.6 %all-to-all-start = ((bf16[4,4,128,512]{2,1,0,3:T(4,128)(2,1)}), bf16[4,4,128,512]{2,1,0,3:T(4,128)(2,1)}, u32[]{:S(2)}, u32[]{:S(2)}) async-start(bf16[4,4,128,512]{2,1,0,3:T(4,128)(2,1)} %copy.26), calls=%async_computation | async-start | bytes 4194304 | tf_op jit(solution)/shard_map/all_to_all | solution.py:30
  48.9 25.1 %all-to-all-done = bf16[4,4,128,512]{2,1,0,3:T(4,128)(2,1)} async-done(((bf16[4,4,128,512]{2,1,0,3:T(4,128)(2,1)}), bf16[4,4,128,512]{2,1,0,3:T(4,128)(2,1)}, u32[]{:S(2)}, u32[]{:S(2)}) %all-to-all-start) | async-done | bytes 2097184 | tf_op jit(solution)/shard_map/all_to_all | solution.py:30
  73.9 3.5 %copy.27 = bf16[4,4,128,512]{2,3,1,0:T(8,128)(2,1)} copy(bf16[4,4,128,512]{2,1,0,3:T(4,128)(2,1)} %all-to-all-done) | data formatting | bytes 4194304 | tf_op jit(solution)/shard_map/all_to_all | solution.py:30
  77.4 4.1 %copy.28 = bf16[4,4,4,128,128]{4,3,2,1,0:T(8,128)(2,1)} copy(bf16[4,4,4,128,128]{3,4,2,1,0:T(8,128)(2,1)} %bitcast.52) | data formatting | bytes 4194304 | tf_op jit(solution)/shard_map/all_to_all | solution.py:30
  81.5 3.7 %gather_fusion = bf16[16,512,128]{2,1,0:T(8,128)(2,1)} fusion(bf16[16,512,128]{2,1,0:T(8,128)(2,1)} %bitcast.51, s32[1024]{0:T(1024)S(1)} %pad_clamp_fusion), kind=kCustom, calls=%fused_computation | custom fusion | bytes 4194368 | tf_op jit(solution)/shard_map/gather | solution.py:42
  85.3 1.8 broadcast_select_fusion
  87.1 53.4 %all_to_all.20 = bf16[8,2,512,128]{3,2,1,0:T(8,128)(2,1)S(1)} all-to-all(bf16[8,2,512,128]{3,2,1,0:T(8,128)(2,1)S(1)} %broadcast_select_fusion), channel_id=1, replica_groups=mesh['super'=8,'col'=4] {'super'}, dimensions={0} | all-to-all | bytes 4194304 | tf_op jit(solution)/shard_map/all_to_all | solution.py:45
  140.5 2.1 fusion
  142.7 1.3 copy.25
  144.0 3.8 %fusion.2 = f32[64,64]{1,0:T(8,128)S(1)} fusion(bf16[4,64,512]{2,1,0:T(8,128)(2,1)S(1)} %copy-done.3, bf16[4,512,512]{2,1,0:T(8,128)(2,1)} %all-gather.2.cloned.1.call-done), kind=kOutput, calls=%fused_computation.12 | convolution fusion | flops 151126016 | bytes 2375680 | tf_op jit(solution)/shard_map/jac,jbc->ab/dot_general | solution.py:26
  147.8 35.1 %psum.15 = f32[64,64]{1,0:T(8,128)S(1)} all-reduce(f32[64,64]{1,0:T(8,128)S(1)} %fusion.2), channel_id=1, replica_groups=mesh['super'=8,'col'=4] {'super'}, use_global_device_ids=true, to_apply=%region_12.13 | all-reduce | flops 4096 | bytes 32768 | tf_op jit(solution)/shard_map/psum | solution.py:29
  183.5 1.5 bitcast_subtract_fusion
  185.0 1.3 copy.30
  186.3 1.4 fusion.3
  188.8 11.7 %cholesky.104 = f32[128,128]{1,0:T(8,128)S(1)} custom-call(f32[128,128]{1,0:T(8,128)S(1)} %cholesky.266), custom_call_target="Cholesky" | custom-call | tf_op jit(solution)/shard_map/jit(cholesky)/cholesky | solution.py:55
  200.5 9.8 %custom-call.27 = f32[1,128,128]{1,2,0:T(8,128)S(1)} custom-call(f32[1,128,128]{2,1,0:T(8,128)S(1)} %get-tuple-element.11), custom_call_target="InvertDiagBlocksLowerTriangular" | custom-call | tf_op jit(solution)/shard_map/jit(cholesky)/cholesky | solution.py:55
  213.0 11.7 %cholesky.217 = f32[128,128]{1,0:T(8,128)S(1)} custom-call(f32[128,128]{1,0:T(8,128)S(1)} %cholesky.270), custom_call_target="Cholesky" | custom-call | tf_op jit(solution)/shard_map/jit(cholesky)/cholesky | solution.py:55
  224.7 10.0 %custom-call.28 = f32[1,128,128]{1,2,0:T(8,128)S(1)} custom-call(f32[1,128,128]{2,1,0:T(8,128)S(1)} %get-tuple-element.8), custom_call_target="InvertDiagBlocksLowerTriangular" | custom-call | tf_op jit(solution)/shard_map/jit(cholesky)/cholesky | solution.py:55
  236.3 11.7 %cholesky.238 = f32[128,128]{1,0:T(8,128)S(1)} custom-call(f32[128,128]{1,0:T(8,128)S(1)} %cholesky.275), custom_call_target="Cholesky" | custom-call | tf_op jit(solution)/shard_map/jit(cholesky)/cholesky | solution.py:55
  248.8 9.8 %custom-call.29 = f32[1,128,128]{1,2,0:T(8,128)S(1)} custom-call(f32[1,128,128]{2,1,0:T(8,128)S(1)} %get-tuple-element.5), custom_call_target="InvertDiagBlocksLowerTriangular" | custom-call | tf_op jit(solution)/shard_map/jit(cholesky)/cholesky | solution.py:55
  260.1 11.7 %cholesky.255 = f32[128,128]{1,0:T(8,128)S(1)} custom-call(f32[128,128]{1,0:T(8,128)S(1)} %convolution_subtract_fusion.2), custom_call_target="Cholesky" | custom-call | tf_op jit(solution)/shard_map/jit(cholesky)/cholesky | solution.py:55
  (44 shorter events, 11.6 us)
Async XLA Ops:
  7.2 27.7 %copy-start = (bf16[4,4,128,512]{3,2,1,0:T(8,128)(2,1)S(1)}, bf16[4,4,128,512]{3,2,1,0:T(8,128)(2,1)}, u32[]{:S(2)}) copy-start(bf16[4,4,128,512]{3,2,1,0:T(8,128)(2,1)} %param.7) | copy-start | bytes 6291460
  7.2 27.7 %all-gather.2.cloned.1.call-start = ((), (), s32[]{:S(2)}) async-start(), calls=%async_computation.2 | async-start | bytes 2621440 | tf_op jit(solution)/shard_map/all_gather | solution.py:16
  43.6 4.6 %copy-start.5 = (s32[4,4]{1,0:T(4,128)S(1)}, s32[4,4]{1,0:T(4,128)}, u32[]{:S(2)}) copy-start(s32[4,4]{1,0:T(4,128)} %param.6) | copy-start | bytes 196
  43.6 30.3 %all-to-all-start = ((bf16[4,4,128,512]{2,1,0,3:T(4,128)(2,1)}), bf16[4,4,128,512]{2,1,0,3:T(4,128)(2,1)}, u32[]{:S(2)}, u32[]{:S(2)}) async-start(bf16[4,4,128,512]{2,1,0,3:T(4,128)(2,1)} %copy.26), calls=%async_computation | async-start | bytes 4194304 | tf_op jit(solution)/shard_map/all_to_all | solution.py:30
  48.2 135.3 %all-reduce.3.cloned.1.call-start = ((), (), s32[]{:S(2)}) async-start(), calls=%async_computation.3 | async-start | bytes 1048576 | tf_op jit(solution)/shard_map/psum | solution.py:52
  140.5 2.1 copy-start.2
  142.6 1.4 copy-start.3
  142.6 40.2 %copy-start.4 = (f32[64,64]{1,0:T(8,128)S(1)}, f32[64,64]{1,0:T(8,128)}, u32[]{:S(2)}) copy-start(f32[64,64]{1,0:T(8,128)} %param.11) | copy-start | bytes 49156
  187.8 1.0 copy-start.1
Sparse Core Ops, SparseCore 0:
  9.6 25.2 all-gather.1
  142.8 31.2 all-reduce.2
where the time goes:
time: 284 us; the launch traced here: 283 us
  blocking collectives  88.5 us (31%)
  other arithmetic  85.3 us (30%)
  waiting for transfers between devices  52.8 us (19%)
  local copies, waits for them, and re-layouts  19.8 us (7%)
  between operations  16.8 us (6%)
  matrix products  15.5 us (5%)
  starting transfers between devices  4.66 us (2%)
    another operation x14, other arithmetic, shards(): factor = jnp.linalg.cholesky(updated)  78.7 us
    all_to_all x1, blocking collectives, shards(): lax.all_to_all(packed, 'super', split_axis=0, concat_axis=0, tiled=True)  53.4 us
    psum x1, blocking collectives, shards(): arrow_total = lax.psum(arrow_local, 'super')  35.1 us
    all_gather x1, waiting for transfers between devices, shards(): portion = lax.all_gather(inv_factors, 'col', axis=1, tiled=True)  27 us
    all_to_all x1, waiting for transfers between devices, shards(): lax.all_to_all(row_panels, 'col', split_axis=3, concat_axis=2, tiled=True)  25.1 us
    all_to_all x2, local copies, waits for them, and re-layouts, shards(): lax.all_to_all(row_panels, 'col', split_axis=3, concat_axis=2, tiled=True)  7.61 us
  transfers between devices with their start and end apart: 3, of which 2 were waited for; matrix products, arithmetic and copies ran while one was open for 2% of the time, Pallas kernels for 0%

commit v1 on v0

v1 whole, which is shorter than its diff:
```python
import functools

import jax
import jax.numpy as jnp
from jax import lax
from jax.experimental import pallas as pl
from jax.experimental.pallas import tpu as pltpu
from jax.sharding import PartitionSpec as P

MESH = pl.DeviceIdType.MESH
EXACT = lax.Precision.HIGHEST
BLK = 128
SUB = 8


def block_pairs(blocks):
    return [(r, c) for r in range(blocks) for c in range(r, blocks)]


def eliminate(rows, extra, step):
    row_ids = lax.broadcasted_iota(jnp.int32, (SUB, BLK), 0)
    base = step * SUB
    cols = [
        jnp.broadcast_to(rows[:, base + b : base + b + 1], (SUB, BLK)) for b in range(SUB)
    ]
    scale = jnp.zeros((SUB, BLK), jnp.float32)
    for m in range(SUB):
        pivot = jnp.broadcast_to(cols[m][m : m + 1], (SUB, BLK))
        inv = lax.rsqrt(pivot)
        scale = jnp.where(row_ids == m, inv, scale)
        if m == SUB - 1:
            break
        low = cols[m] * inv
        for b in range(m + 1, SUB):
            cols[b] = cols[b] - low * jnp.broadcast_to(low[b : b + 1], (SUB, BLK))
        low = jnp.where(row_ids > m, low * inv, 0.0)
        rows = rows - low * jnp.broadcast_to(rows[m : m + 1], (SUB, BLK))
        if extra is not None:
            extra = extra - low * jnp.broadcast_to(extra[m : m + 1], (SUB, BLK))
    return rows * scale, None if extra is None else extra * scale


def cholesky_kernel(target_ref, total_ref, out_ref, u_ref, d_ref, q_ref):
    blocks = target_ref.shape[1] // BLK
    pairs = block_pairs(blocks)
    row_ids = lax.broadcasted_iota(jnp.int32, (BLK, BLK), 0)
    col_ids = lax.broadcasted_iota(jnp.int32, (BLK, BLK), 1)
    for kb in range(blocks):
        lo = kb * BLK
        update = None
        if kb:
            update = lax.dot_general(
                u_ref[0:lo, lo : lo + BLK],
                u_ref[0:lo, lo:],
                (((0,), (0,)), ((), ())),
                precision=EXACT,
                preferred_element_type=jnp.float32,
            )
        panel = []
        for cb in range(kb, blocks):
            part = target_ref[0, lo : lo + BLK, cb * BLK : (cb + 1) * BLK]
            part = part - total_ref[pairs.index((kb, cb))].astype(jnp.float32)
            if kb:
                part = part - update[:, (cb - kb) * BLK : (cb - kb + 1) * BLK]
            panel.append(part)
        last = kb == blocks - 1
        d_ref[...] = panel[0]
        if not last:
            q_ref[...] = (row_ids == col_ids).astype(jnp.float32)
        steps = BLK // SUB
        for step in range(steps):
            here = slice(step * SUB, (step + 1) * SUB)
            rows, extra = eliminate(d_ref[here], None if last else q_ref[here], step)
            d_ref[here] = rows
            if not last:
                q_ref[here] = extra
            if step < steps - 1:
                below = slice((step + 1) * SUB, BLK)
                right = rows if last else jnp.concatenate([rows, extra], axis=1)
                change = lax.dot_general(
                    rows,
                    right,
                    (((0,), (0,)), ((), ())),
                    precision=EXACT,
                    preferred_element_type=jnp.float32,
                )
                d_ref[below] = d_ref[below] - change[below, :BLK]
                if not last:
                    q_ref[below] = q_ref[below] - change[below, BLK:]
        u_ref[lo : lo + BLK, lo : lo + BLK] = jnp.where(row_ids <= col_ids, d_ref[...], 0.0)
        if not last:
            u_ref[lo : lo + BLK, lo + BLK :] = jnp.dot(
                q_ref[...],
                jnp.concatenate(panel[1:], axis=1),
                precision=EXACT,
                preferred_element_type=jnp.float32,
            )
    me = lax.axis_index("col")
    for mine in range(blocks):

        @pl.when(me == mine)
        def _():
            for b in range(blocks):
                there = slice(b * BLK, (b + 1) * BLK)
                if b <= mine:
                    out_ref[0, :, there] = u_ref[there, mine * BLK : (mine + 1) * BLK].T
                else:
                    out_ref[0, :, there] = jnp.zeros((BLK, BLK), jnp.float32)


def factor_rows(target_blocks, total):
    width = target_blocks.shape[1]
    vmem = pl.BlockSpec(memory_space=pltpu.VMEM)
    return pl.pallas_call(
        cholesky_kernel,
        out_shape=jax.ShapeDtypeStruct((1, BLK, width), jnp.float32),
        in_specs=[vmem, vmem],
        out_specs=vmem,
        scratch_shapes=[
            pltpu.VMEM((width, width), jnp.float32),
            pltpu.VMEM((BLK, BLK), jnp.float32),
            pltpu.VMEM((BLK, BLK), jnp.float32),
        ],
        compiler_params=pltpu.CompilerParams(vmem_limit_bytes=24 * 2**20),
        name="factor",
    )(target_blocks, total)

def routed(parent, off_blocks, inv_factors, arrow_rows):
    supers = lax.axis_size("super")
    sources, fanout, slab_rows, block_width = off_blocks.shape
    item_count = sources * fanout
    capacity = max(2, (item_count + supers - 1) // supers)
    stacked_rows = off_blocks.reshape(sources, fanout * slab_rows, block_width)
    portion = lax.all_gather(inv_factors, "col", axis=1, tiled=True)
    rows_part = jnp.einsum(
        "jrk,jck->jrc", stacked_rows, portion, preferred_element_type=jnp.float32
    ).astype(jnp.bfloat16)
    arrow_panels = jnp.einsum(
        "jak,jck->jac", arrow_rows, portion, preferred_element_type=jnp.float32
    ).astype(jnp.bfloat16)
    arrow_local = jnp.einsum(
        "jac,jbc->ab", arrow_panels, arrow_panels, preferred_element_type=jnp.float32
    )
    arrow_total = lax.psum(arrow_local, "super")
    row_panels = rows_part.reshape(sources, fanout, slab_rows, block_width)
    panels = lax.all_to_all(row_panels, "col", split_axis=3, concat_axis=2, tiled=True)
    column_panels = panels.reshape(item_count, block_width, panels.shape[3])
    owners = parent.reshape(item_count)
    item_index = jnp.arange(item_count, dtype=jnp.int32)
    matching = owners[:, None] == owners[None, :]
    earlier = item_index[None, :] < item_index[:, None]
    position = jnp.sum((matching & earlier).astype(jnp.int32), axis=1)
    target_slot = owners * capacity + position
    slots = jnp.arange(supers * capacity, dtype=jnp.int32)
    chosen = (slots[:, None] == target_slot[None, :]).astype(jnp.bfloat16)
    packed = jnp.einsum(
        "pi,irc->prc", chosen, column_panels, preferred_element_type=jnp.float32
    ).astype(jnp.bfloat16)
    packed = packed.reshape(supers, capacity, block_width, column_panels.shape[2])
    received = lax.all_to_all(packed, "super", split_axis=0, concat_axis=0, tiled=True)
    schur_local = jnp.einsum(
        "dmrc,dmsc->rs", received, received, preferred_element_type=jnp.float32
    )
    schur = lax.psum(schur_local.astype(jnp.bfloat16), "col")
    blocks = block_width // BLK
    total = jnp.stack(
        [
            schur[r * BLK : (r + 1) * BLK, c * BLK : (c + 1) * BLK]
            for r, c in block_pairs(blocks)
        ]
    )
    return total, arrow_total


def shards(parent, off_blocks, inv_factors, arrow_rows, target_blocks, arrow_block):
    total, arrow_total = routed(parent, off_blocks, inv_factors, arrow_rows)
    return factor_rows(target_blocks, total), arrow_block - arrow_total


def solution(mesh):
    placed = (
        P("super", None),
        P("super", None, "col", None),
        P("super", "col", None),
        P("super", None, None),
        P("super", None, None),
        P(),
    )
    return jax.shard_map(
        shards,
        mesh=mesh,
        in_specs=placed,
        out_specs=(P("super", "col", None), P()),
        check_vma=False,
    )
```

time: 284 us -> 230 us (0.81)
  other arithmetic: 85.3 us -> 0.81 us
  Pallas kernels: 0 us -> 35.7 us
  matrix products: 15.5 us -> 12.4 us
    another operation x14 -> x0, other arithmetic: 78.7 us -> none  [shards(): factor = jnp.linalg.cholesky(updated)]
    pallas_call x0 -> x1, Pallas kernels: none -> 35.7 us  [factor_rows(): pl.pallas_call(cholesky_kernel, out_shape=jax.ShapeDtypeStruct((1, BLK, w...]
    another operation x6 -> x0, matrix products: 5.46 us -> none  [shards(): factor = jnp.linalg.cholesky(updated)]
    unnamed x13 -> x19, local copies, waits for them, and re-layouts: 2.33 us -> 6.91 us
    gather x1 -> x0, local copies, waits for them, and re-layouts: 3.73 us -> none  [shards(): column_panels[source_item]]
    dot_general x3 -> x4, matrix products: 10 us -> 12.4 us  [the longest x1 4.18 us: routed(): jnp.einsum('jrk,jck->jrc', stacked_rows, portion, preferred_element_type=...]
    all_to_all x2 -> x1, local copies, waits for them, and re-layouts: 7.61 us -> 6.5 us  [routed(): lax.all_to_all(row_panels, 'col', split_axis=3, concat_axis=2, tiled=True)]
where the time goes in v1:
time: 230 us; the launch traced here: 229 us
  blocking collectives  88.5 us (38%)
  waiting for transfers between devices  53.1 us (23%)
  Pallas kernels  35.7 us (16%)
  local copies, waits for them, and re-layouts  19.3 us (8%)
  between operations  14.1 us (6%)
  matrix products  12.4 us (5%)
  starting transfers between devices  4.65 us (2%)
    all_to_all x1, blocking collectives, routed(): lax.all_to_all(packed, 'super', split_axis=0, concat_axis=0, tiled=True)  53.4 us
    pallas_call x1, Pallas kernels, factor_rows(): pl.pallas_call(cholesky_kernel, out_shape=jax.ShapeDtypeStruct((1, BLK, w...  35.7 us
    psum x1, blocking collectives, routed(): arrow_total = lax.psum(arrow_local, 'super')  35.1 us
    all_gather x1, waiting for transfers between devices, routed(): portion = lax.all_gather(inv_factors, 'col', axis=1, tiled=True)  27 us
    all_to_all x1, waiting for transfers between devices, routed(): lax.all_to_all(row_panels, 'col', split_axis=3, concat_axis=2, tiled=True)  25.4 us
    unnamed x19, local copies, waits for them, and re-layouts  6.91 us
    all_to_all x1, local copies, waits for them, and re-layouts, routed(): lax.all_to_all(row_panels, 'col', split_axis=3, concat_axis=2, tiled=True)  6.5 us
  transfers between devices with their start and end apart: 3, of which 2 were waited for; matrix products, arithmetic and copies ran while one was open for 2% of the time, Pallas kernels for 0%

profile of v1, /device:TPU:0, one launch (start us, length us, event | category | flops | bytes accessed | tf_op | source)
XLA Modules:
  0.0 228.6 jit_solution(11916821594942116670)
XLA Ops:
  7.2 0.7 all-gather.2.cloned.1.call-update
  7.9 27.0 %all-gather.2.cloned.1.call-done = bf16[4,512,512]{2,1,0:T(8,128)(2,1)} async-done(((bf16[4,128,512]{2,1,0:T(8,128)(2,1)}), bf16[4,512,512]{2,1,0:T(8,128)(2,1)}) %all-gather.2.cloned.1.call-update) | async-done | bytes 2097168 | tf_op jit(solution)/shard_map/all_gather | solution.py:134
  34.9 4.2 %convolution_convert_fusion.1 = bf16[4,512,512]{2,1,0:T(8,128)(2,1)} fusion(bf16[4,512,512]{2,1,0:T(8,128)(2,1)S(1)} %bitcast.65, bf16[4,512,512]{2,1,0:T(8,128)(2,1)} %all-gather.2.cloned.1.call-done), kind=kOutput, calls=%fused_computation.1 | convolution fusion | flops 1074790400 | bytes 6291456 | tf_op jit(solution)/shard_map/jrk,jck->jrc/dot_general | solution.py:135
  39.1 4.5 %copy.13 = bf16[4,4,128,512]{2,1,0,3:T(4,128)(2,1)} copy(bf16[4,4,128,512]{3,2,1,0:T(8,128)(2,1)} %bitcast.68) | data formatting | bytes 4194304 | tf_op jit(solution)/shard_map/reshape | solution.py:145
  43.6 4.6 %all-to-all-start = ((bf16[4,4,128,512]{2,1,0,3:T(4,128)(2,1)}), bf16[4,4,128,512]{2,1,0,3:T(4,128)(2,1)}, u32[]{:S(2)}, u32[]{:S(2)}) async-start(bf16[4,4,128,512]{2,1,0,3:T(4,128)(2,1)} %copy.13), calls=%async_computation | async-start | bytes 4194304 | tf_op jit(solution)/shard_map/all_to_all | solution.py:146
  48.5 25.4 %all-to-all-done = bf16[4,4,128,512]{2,1,0,3:T(4,128)(2,1)} async-done(((bf16[4,4,128,512]{2,1,0,3:T(4,128)(2,1)}), bf16[4,4,128,512]{2,1,0,3:T(4,128)(2,1)}, u32[]{:S(2)}, u32[]{:S(2)}) %all-to-all-start) | async-done | bytes 2097184 | tf_op jit(solution)/shard_map/all_to_all | solution.py:146
  74.0 6.5 %copy.14 = bf16[4,4,128,4,128]{4,1,0,2,3:T(4,128)(2,1)} copy(bf16[4,4,128,4,128]{2,1,0,4,3:T(4,128)(2,1)} %bitcast.3) | data formatting | bytes 4194304 | tf_op jit(solution)/shard_map/all_to_all | solution.py:146
  80.4 2.3 convolution_convert_fusion
  83.3 53.4 %all_to_all.20 = bf16[8,2,512,128]{3,2,1,0:T(8,128)(2,1)S(1)} all-to-all(bf16[8,2,512,128]{3,2,1,0:T(8,128)(2,1)S(1)} %copy.15), channel_id=1, replica_groups=mesh['super'=8,'col'=4] {'super'}, dimensions={0} | all-to-all | bytes 4194304 | tf_op jit(solution)/shard_map/all_to_all | solution.py:160
  136.7 2.1 fusion
  138.9 3.9 %fusion.2 = f32[64,64]{1,0:T(8,128)S(1)} fusion(bf16[4,64,512]{2,1,0:T(8,128)(2,1)S(1)} %copy-done.2, bf16[4,512,512]{2,1,0:T(8,128)(2,1)} %all-gather.2.cloned.1.call-done), kind=kOutput, calls=%fused_computation.6 | convolution fusion | flops 151126016 | bytes 2375680 | tf_op jit(solution)/shard_map/jac,jbc->ab/dot_general | solution.py:141
  142.7 35.1 %psum.15 = f32[64,64]{1,0:T(8,128)S(1)} all-reduce(f32[64,64]{1,0:T(8,128)S(1)} %fusion.2), channel_id=1, replica_groups=mesh['super'=8,'col'=4] {'super'}, use_global_device_ids=true, to_apply=%region_2.0 | all-reduce | flops 4096 | bytes 32768 | tf_op jit(solution)/shard_map/psum | solution.py:144
  177.8 0.6 sub.3
  178.4 0.8 fusion.12
  179.2 0.8 fusion.11
  180.0 0.8 fusion.10
  180.7 0.8 fusion.9
  181.5 0.8 fusion.8
  182.3 0.8 fusion.7
  183.0 0.8 fusion.6
  183.8 0.8 fusion.5
  184.6 0.8 fusion.4
  185.3 0.8 fusion.3.total_ref
  186.1 35.7 %factor.1 = f32[1,128,512]{2,1,0:T(8,128)} custom-call(f32[1,512,512]{2,1,0:T(8,128)S(1)} %copy-done.1, bf16[10,128,128]{2,1,0:T(8,128)(2,1)S(1)} %fusion.3.total_ref), custom_call_target="tpu_custom_call" | custom-call | tf_op jit(solution)/shard_map/factor/pallas_call | solution.py:114
  (18 shorter events, 0.9 us)
Async XLA Ops:
  7.2 27.7 %copy-start = (bf16[4,4,128,512]{3,2,1,0:T(8,128)(2,1)S(1)}, bf16[4,4,128,512]{3,2,1,0:T(8,128)(2,1)}, u32[]{:S(2)}) copy-start(bf16[4,4,128,512]{3,2,1,0:T(8,128)(2,1)} %param.7) | copy-start | bytes 6291460
  7.2 27.7 %all-gather.2.cloned.1.call-start = ((), (), s32[]{:S(2)}) async-start(), calls=%async_computation.2 | async-start | bytes 2621440 | tf_op jit(solution)/shard_map/all_gather | solution.py:134
  43.6 4.6 %copy-start.4 = (s32[4,4]{1,0:T(4,128)S(1)}, s32[4,4]{1,0:T(4,128)}, u32[]{:S(2)}) copy-start(s32[4,4]{1,0:T(4,128)} %param.6) | copy-start | bytes 196
  43.6 30.3 %all-to-all-start = ((bf16[4,4,128,512]{2,1,0,3:T(4,128)(2,1)}), bf16[4,4,128,512]{2,1,0,3:T(4,128)(2,1)}, u32[]{:S(2)}, u32[]{:S(2)}) async-start(bf16[4,4,128,512]{2,1,0,3:T(4,128)(2,1)} %copy.13), calls=%async_computation | async-start | bytes 4194304 | tf_op jit(solution)/shard_map/all_to_all | solution.py:146
  48.2 130.2 %all-reduce.2.cloned.1.call-start = ((), (), s32[]{:S(2)}) async-start(), calls=%async_computation.3 | async-start | bytes 1048576 | tf_op jit(solution)/shard_map/psum | solution.py:164
  136.7 2.1 copy-start.2
  138.8 39.0 %copy-start.3 = (f32[64,64]{1,0:T(8,128)S(1)}, f32[64,64]{1,0:T(8,128)}, u32[]{:S(2)}) copy-start(f32[64,64]{1,0:T(8,128)} %param.11) | copy-start | bytes 49156
  138.8 47.3 %copy-start.1 = (f32[1,512,512]{2,1,0:T(8,128)S(1)}, f32[1,512,512]{2,1,0:T(8,128)}, u32[]{:S(2)}) copy-start(f32[1,512,512]{2,1,0:T(8,128)} %target_ref.1) | copy-start | bytes 3145732
Sparse Core Ops, SparseCore 0:
  9.6 25.2 all-gather.1
  139.0 31.1 all-reduce.1

commit v2 on v1

--- a/solution.py
+++ b/solution.py
@@ -172,9 +172,272 @@
     return total, arrow_total
 
 
+def exchange_kernel(
+    supers, cols, fanout,
+    parent_ref, off_ref, inv_ref, arrow_rows_ref, arrow_block_ref,
+    total_ref, arrow_ref,
+    inv_all, outgoing, off_all, panel, sums, landed, arrow_all, total,
+    inv_send, inv_recv, off_send, off_recv, sum_send, sum_recv,
+    arrow_send, arrow_recv, cast_send, cast_recv,
+):
+    sources = inv_ref.shape[0]
+    slab = inv_ref.shape[1]
+    width = inv_ref.shape[2]
+    blocks = width // BLK
+    pairs = block_pairs(blocks)
+    rounds = supers // cols
+    me_s, me_c = lax.axis_index("super"), lax.axis_index("col")
+    y, core = lax.div(me_c, 2), lax.rem(me_c, 2)
+    beside = 2 * y + 1 - core
+    across = 2 * (1 - y) + core
+    diagonal = 2 * (1 - y) + 1 - core
+    peers = (beside, across, diagonal)
+
+    barrier = pltpu.get_barrier_semaphore()
+    for peer in peers:
+        pl.semaphore_signal(
+            barrier, inc=1, device_id={"super": me_s, "col": peer}, device_id_type=MESH
+        )
+    for d in range(1, supers):
+        pl.semaphore_signal(
+            barrier,
+            inc=1,
+            device_id={"super": lax.rem(me_s + d, supers), "col": me_c},
+            device_id_type=MESH,
+        )
+    pl.semaphore_wait(barrier, cols - 1 + supers - 1)
+
+    def remote(src, dst, send, recv, sup, col):
+        return pltpu.make_async_remote_copy(
+            src_ref=src,
+            dst_ref=dst,
+            send_sem=send,
+            recv_sem=recv,
+            device_id={"super": sup, "col": col},
+            device_id_type=MESH,
+        )
+
+    inv_across = remote(inv_ref, inv_all.at[:, me_c], inv_send.at[1], inv_recv.at[1], me_s, across)
+    inv_across.start()
+    inv_beside = remote(inv_ref, inv_all.at[:, me_c], inv_send.at[0], inv_recv.at[0], me_s, beside)
+    inv_beside.start()
+
+    entries = [
+        (parent_ref[j, t], j * fanout + t, j) for j in range(sources) for t in range(fanout)
+    ]
+    half = lax.div(me_s, cols)
+
+    def parent_of(col, t):
+        return col + cols * lax.rem(half + 1 + t, rounds)
+
+    def items(col, t):
+        p = parent_of(col, t)
+        first, first_source = jnp.int32(len(entries) - 1), jnp.int32(sources - 1)
+        second, second_source = jnp.int32(0), jnp.int32(0)
+        for owner, item, source in entries:
+            hit = owner == p
+            first = jnp.where(hit, jnp.minimum(first, item), first)
+            first_source = jnp.where(hit, jnp.minimum(first_source, source), first_source)
+            second = jnp.where(hit, item, second)
+            second_source = jnp.where(hit, source, second_source)
+        return (first, second), (first_source, second_source)
+
+    off_copies = {}
+    own_sources = []
+    for t in range(rounds):
+        for k in (1, 2, 0):
+            chosen, _ = items(peers[k], t)
+            for m in range(2):
+                outgoing[k, t, m] = off_ref[chosen[m]]
+            copy = remote(
+                outgoing.at[k, t],
+                off_all.at[t, :, me_c],
+                off_send.at[k, t],
+                off_recv.at[k, t],
+                me_s,
+                peers[k],
+            )
+            copy.start()
+            off_copies[k, t] = copy
+        chosen, chosen_sources = items(me_c, t)
+        own_sources.append(chosen_sources)
+        for m in range(2):
+            off_all[t, m, me_c] = off_ref[chosen[m]]
+    for j in range(sources):
+        inv_all[j, me_c] = inv_ref[j]
+
+    inv_across.wait_recv()
+    inv_onward = remote(
+        inv_all.at[:, across], inv_all.at[:, across], inv_send.at[2], inv_recv.at[2], me_s, beside
+    )
+    inv_onward.start()
+    inv_beside.wait_recv()
+    inv_onward.wait_recv()
+
+    nt = (((1,), (1,)), ((), ()))
+    arrow_sum = jnp.zeros(arrow_ref.shape, jnp.float32)
+    for j in range(sources):
+        rows = lax.dot_general(
+            arrow_rows_ref[j],
+            inv_all[j].reshape(width, width),
+            nt,
+            preferred_element_type=jnp.float32,
+        ).astype(jnp.bfloat16)
+        arrow_sum = arrow_sum + lax.dot_general(
+            rows, rows, nt, preferred_element_type=jnp.float32
+        )
+    arrow_all[me_s] = arrow_sum
+    arrow_copies = []
+    for d in range(1, supers):
+        copy = remote(
+            arrow_all.at[me_s],
+            arrow_all.at[me_s],
+            arrow_send.at[d],
+            arrow_recv.at[d],
+            lax.rem(me_s + d, supers),
+            me_c,
+        )
+        copy.start()
+        arrow_copies.append(copy)
+
+    for t in range(rounds):
+        for k in range(3):
+            off_copies[k, t].wait_recv()
+        for m in range(2):
+            panel[:, m * width : (m + 1) * width] = lax.dot_general(
+                off_all[t, m].reshape(width, width),
+                inv_all[own_sources[t][m]].reshape(width, width),
+                nt,
+                preferred_element_type=jnp.float32,
+            ).astype(jnp.bfloat16)
+        for r in range(blocks):
+            product = lax.dot_general(
+                panel[r * BLK : (r + 1) * BLK, :],
+                panel[r * BLK :, :],
+                nt,
+                preferred_element_type=jnp.float32,
+            ).astype(jnp.bfloat16)
+            for c in range(r, blocks):
+                sums[t, pairs.index((r, c))] = product[:, (c - r) * BLK : (c - r + 1) * BLK]
+        p = parent_of(me_c, t)
+
+        @pl.when(p != me_s)
+        def _():
+            remote(
+                sums.at[t], landed.at[me_s], sum_send.at[t], sum_recv.at[me_s], p, me_c
+            ).start()
+
+        @pl.when(p == me_s)
+        def _():
+            landed[me_s] = sums[t]
+
+    chief = lax.rem(me_s, cols)
+
+    def cast(n, col):
+        return remote(total, total, cast_send.at[n], cast_recv.at[0], me_s, col)
+
+    @pl.when(me_c == chief)
+    def _():
+        for d in range(1, supers):
+            s = lax.rem(me_s + d, supers)
+            remote(
+                sums.at[0], landed.at[s], sum_send.at[0], sum_recv.at[s], me_s, beside
+            ).wait_recv()
+        for b in range(len(pairs)):
+            acc = landed[0, b].astype(jnp.float32)
+            for s in range(1, supers):
+                acc = acc + landed[s, b].astype(jnp.float32)
+            total[b] = acc.astype(jnp.bfloat16)
+        first, second = cast(0, across), cast(1, beside)
+        first.start()
+        second.start()
+        first.wait_send()
+        second.wait_send()
+
+    @pl.when(me_c != chief)
+    def _():
+        cast(0, beside).wait_recv()
+
+    @pl.when(across == chief)
+    def _():
+        onward = cast(1, beside)
+        onward.start()
+        onward.wait_send()
+
+    total_ref[...] = total[...]
+
+    for copy in arrow_copies:
+        copy.wait_recv()
+    arrow_total = arrow_all[0]
+    for s in range(1, supers):
+        arrow_total = arrow_total + arrow_all[s]
+    arrow_ref[...] = arrow_block_ref[...] - arrow_total
+
+    for copy in (inv_across, inv_beside, inv_onward, *off_copies.values(), *arrow_copies):
+        copy.wait_send()
+    for t in range(rounds):
+        p = parent_of(me_c, t)
+
+        @pl.when(p != me_s)
+        def _():
+            remote(
+                sums.at[t], landed.at[me_s], sum_send.at[t], sum_recv.at[me_s], p, me_c
+            ).wait_send()
+
+
+def exchanged(parent, off_blocks, inv_factors, arrow_rows, arrow_block):
+    supers, cols = lax.axis_size("super"), lax.axis_size("col")
+    sources, fanout, slab, width = off_blocks.shape
+    arrow = arrow_block.shape[0]
+    rounds = supers // cols
+    count = len(block_pairs(width // BLK))
+    vmem = pl.BlockSpec(memory_space=pltpu.VMEM)
+    bf16, f32 = jnp.bfloat16, jnp.float32
+    dma = pltpu.SemaphoreType.DMA
+    return pl.pallas_call(
+        functools.partial(exchange_kernel, supers, cols, fanout),
+        out_shape=(
+            jax.ShapeDtypeStruct((count, BLK, BLK), bf16),
+            jax.ShapeDtypeStruct((arrow, arrow), f32),
+        ),
+        in_specs=[pl.BlockSpec(memory_space=pltpu.SMEM)] + [vmem] * 4,
+        out_specs=(vmem, vmem),
+        scratch_shapes=[
+            pltpu.VMEM((sources, cols, slab, width), bf16),
+            pltpu.VMEM((cols - 1, rounds, 2, slab, width), bf16),
+            pltpu.VMEM((rounds, 2, cols, slab, width), bf16),
+            pltpu.VMEM((width, 2 * width), bf16),
+            pltpu.VMEM((rounds, count, BLK, BLK), bf16),
+            pltpu.VMEM((supers, count, BLK, BLK), bf16),
+            pltpu.VMEM((supers, arrow, arrow), f32),
+            pltpu.VMEM((count, BLK, BLK), bf16),
+            dma((3,)),
+            dma((3,)),
+            dma((3, rounds)),
+            dma((3, rounds)),
+            dma((rounds,)),
+            dma((supers,)),
+            dma((supers,)),
+            dma((supers,)),
+            dma((2,)),
+            dma((1,)),
+        ],
+        compiler_params=pltpu.CompilerParams(
+            collective_id=0, has_side_effects=True, vmem_limit_bytes=40 * 2**20
+        ),
+        name="exchange",
+    )(parent, off_blocks.reshape(sources * fanout, slab, width), inv_factors, arrow_rows, arrow_block)
+
+
 def shards(parent, off_blocks, inv_factors, arrow_rows, target_blocks, arrow_block):
-    total, arrow_total = routed(parent, off_blocks, inv_factors, arrow_rows)
-    return factor_rows(target_blocks, total), arrow_block - arrow_total
+    supers, cols = lax.axis_size("super"), lax.axis_size("col")
+    entries = off_blocks.shape[0] * off_blocks.shape[1]
+    if cols == 4 and supers == 2 * cols and entries == 2 * supers:
+        total, arrow_update = exchanged(parent, off_blocks, inv_factors, arrow_rows, arrow_block)
+    else:
+        total, arrow_total = routed(parent, off_blocks, inv_factors, arrow_rows)
+        arrow_update = arrow_block - arrow_total
+    return factor_rows(target_blocks, total), arrow_update
 
 
 def solution(mesh):

time: 230 us -> 104 us (0.45)
  blocking collectives: 88.5 us -> 0 us
  Pallas kernels: 35.7 us -> 95.7 us
  waiting for transfers between devices: 53.1 us -> 0 us
  local copies, waits for them, and re-layouts: 19.3 us -> 5.63 us
  between operations: 14.1 us -> 0.66 us
  matrix products: 12.4 us -> 0 us
  starting transfers between devices: 4.65 us -> 0 us
    pallas_call x0 -> x1, Pallas kernels: none -> 59.9 us  [exchanged(): pl.pallas_call(functools.partial(exchange_kernel, supers, cols, fanout),...]
    all_to_all x1 -> x0, blocking collectives: 53.4 us -> none  [routed(): lax.all_to_all(packed, 'super', split_axis=0, concat_axis=0, tiled=True)]
    psum x1 -> x0, blocking collectives: 35.1 us -> none  [routed(): arrow_total = lax.psum(arrow_local, 'super')]
    all_gather x1 -> x0, waiting for transfers between devices: 27 us -> none  [routed(): portion = lax.all_gather(inv_factors, 'col', axis=1, tiled=True)]
    all_to_all x1 -> x0, waiting for transfers between devices: 25.4 us -> none  [routed(): lax.all_to_all(row_panels, 'col', split_axis=3, concat_axis=2, tiled=True)]
    dot_general x4 -> x0, matrix products: 12.4 us -> none  [the longest x1 4.18 us: routed(): jnp.einsum('jrk,jck->jrc', stacked_rows, portion, preferred_element_type=...]
    all_to_all x1 -> x0, local copies, waits for them, and re-layouts: 6.5 us -> none  [routed(): lax.all_to_all(row_panels, 'col', split_axis=3, concat_axis=2, tiled=True)]
    reshape x3 -> x0, local copies, waits for them, and re-layouts: 5.15 us -> none  [the longest x1 4.52 us: routed(): row_panels = rows_part.reshape(sources, fanout, slab_rows, block_width)]
  transfers between devices with their start and end apart: 3 -> 0, of which waited for: 2 -> 0; matrix products, arithmetic and copies ran while one was open for 2% -> 0% of each run, Pallas kernels for 0% -> 0%
where the time goes in v2:
time: 104 us; the launch traced here: 102 us
  Pallas kernels  95.7 us (92%)
  local copies, waits for them, and re-layouts  5.63 us (5%)
    pallas_call x1, Pallas kernels, exchanged(): pl.pallas_call(functools.partial(exchange_kernel, supers, cols, fanout),...  59.9 us
    pallas_call x1, Pallas kernels, factor_rows(): pl.pallas_call(cholesky_kernel, out_shape=jax.ShapeDtypeStruct((1, BLK, w...  35.7 us
    unnamed x13, local copies, waits for them, and re-layouts  5.63 us

profile of v2, /device:TPU:0, one launch (start us, length us, event | category | flops | bytes accessed | tf_op | source)
XLA Modules:
  0.0 102.0 jit_solution(16526224215766042581)
XLA Ops:
  0.6 0.0 copy-start
  0.6 1.6 %copy-done = bf16[4,4,128,512]{3,2,1,0:T(8,128)(2,1)S(1)} copy-done((bf16[4,4,128,512]{3,2,1,0:T(8,128)(2,1)S(1)}, bf16[4,4,128,512]{3,2,1,0:T(8,128)(2,1)}, u32[]{:S(2)}) %copy-start) | copy-done | bytes 2097176
  2.2 0.0 copy-start.2
  2.2 1.0 %copy-done.2 = bf16[4,128,512]{2,1,0:T(8,128)(2,1)S(1)} copy-done((bf16[4,128,512]{2,1,0:T(8,128)(2,1)S(1)}, bf16[4,128,512]{2,1,0:T(8,128)(2,1)}, u32[]{:S(2)}) %copy-start.2) | copy-done | bytes 524312
  3.3 0.0 copy-start.3
  3.3 0.9 copy-done.3
  4.2 0.0 copy-start.4
  4.2 0.8 copy-done.4
  5.0 0.0 copy-start.5
  5.0 0.7 copy-done.5
  5.7 0.0 copy-start.1
  5.7 59.9 %exchange.1 = (bf16[10,128,128]{2,1,0:T(8,128)(2,1)S(1)}, f32[64,64]{1,0:T(8,128)S(1)}) custom-call(s32[4,4]{1,0:T(4,128)S(1)} %copy-done.5, bf16[16,128,512]{2,1,0:T(8,128)(2,1)S(1)} %bitcast.1, bf16[4,128,512]{2,1,0:T(8,128)(2,1)S(1)} %copy-done.2, bf16[4,64,512]{2,1,0:T(8,128)(2,1)S(1)} %copy-done.3, f32[64,64]{1,0:T(8,128)S(1)} %copy-done.4), custom_call_target="tpu_custom_call" | custom-call | tf_op jit(solution)/shard_map/exchange/pallas_call | solution.py:397
  65.6 0.0 copy-done.1
  65.6 35.7 %factor.1 = f32[1,128,512]{2,1,0:T(8,128)} custom-call(f32[1,512,512]{2,1,0:T(8,128)S(1)} %copy-done.1, bf16[10,128,128]{2,1,0:T(8,128)(2,1)S(1)} %get-tuple-element.4.total_ref), custom_call_target="tpu_custom_call" | custom-call | tf_op jit(solution)/shard_map/factor/pallas_call | solution.py:114
  101.4 0.6 copy.9
Async XLA Ops:
  0.6 1.6 %copy-start = (bf16[4,4,128,512]{3,2,1,0:T(8,128)(2,1)S(1)}, bf16[4,4,128,512]{3,2,1,0:T(8,128)(2,1)}, u32[]{:S(2)}) copy-start(bf16[4,4,128,512]{3,2,1,0:T(8,128)(2,1)} %param.7) | copy-start | bytes 6291460
  2.2 1.0 %copy-start.2 = (bf16[4,128,512]{2,1,0:T(8,128)(2,1)S(1)}, bf16[4,128,512]{2,1,0:T(8,128)(2,1)}, u32[]{:S(2)}) copy-start(bf16[4,128,512]{2,1,0:T(8,128)(2,1)} %inv_ref.1) | copy-start | bytes 1572868
  3.3 0.9 copy-start.3
  4.2 0.8 copy-start.4
  5.0 0.7 copy-start.5
  5.7 60.0 %copy-start.1 = (f32[1,512,512]{2,1,0:T(8,128)S(1)}, f32[1,512,512]{2,1,0:T(8,128)}, u32[]{:S(2)}) copy-start(f32[1,512,512]{2,1,0:T(8,128)} %target_ref.1) | copy-start | bytes 3145732

commit v3 on v2

--- a/solution.py
+++ b/solution.py
@@ -10,11 +10,27 @@
 MESH = pl.DeviceIdType.MESH
 EXACT = lax.Precision.HIGHEST
 BLK = 128
-SUB = 8
+SUB = 16
 
 
 def block_pairs(blocks):
     return [(r, c) for r in range(blocks) for c in range(r, blocks)]
+
+
+def halves(x):
+    high = x.astype(jnp.bfloat16)
+    return high, (x - high.astype(jnp.float32)).astype(jnp.bfloat16)
+
+
+def thin_product(a, b):
+    a_high, a_low = halves(a)
+    b_high, b_low = halves(b)
+    return lax.dot_general(
+        jnp.concatenate([a_high, a_high, a_low], axis=0),
+        jnp.concatenate([b_high, b_low, b_high], axis=0),
+        (((0,), (0,)), ((), ())),
+        preferred_element_type=jnp.float32,
+    )
 
 
 def eliminate(rows, extra, step):
@@ -40,8 +56,8 @@
     return rows * scale, None if extra is None else extra * scale
 
 
-def cholesky_kernel(target_ref, total_ref, out_ref, u_ref, d_ref, q_ref):
-    blocks = target_ref.shape[1] // BLK
+def cholesky_kernel(updated_ref, out_ref, u_ref, d_ref, q_ref):
+    blocks = out_ref.shape[2] // BLK
     pairs = block_pairs(blocks)
     row_ids = lax.broadcasted_iota(jnp.int32, (BLK, BLK), 0)
     col_ids = lax.broadcasted_iota(jnp.int32, (BLK, BLK), 1)
@@ -58,8 +74,7 @@
             )
         panel = []
         for cb in range(kb, blocks):
-            part = target_ref[0, lo : lo + BLK, cb * BLK : (cb + 1) * BLK]
-            part = part - total_ref[pairs.index((kb, cb))].astype(jnp.float32)
+            part = updated_ref[pairs.index((kb, cb))]
             if kb:
                 part = part - update[:, (cb - kb) * BLK : (cb - kb + 1) * BLK]
             panel.append(part)
@@ -77,13 +92,7 @@
             if step < steps - 1:
                 below = slice((step + 1) * SUB, BLK)
                 right = rows if last else jnp.concatenate([rows, extra], axis=1)
-                change = lax.dot_general(
-                    rows,
-                    right,
-                    (((0,), (0,)), ((), ())),
-                    precision=EXACT,
-                    preferred_element_type=jnp.float32,
-                )
+                change = thin_product(rows, right)
                 d_ref[below] = d_ref[below] - change[below, :BLK]
                 if not last:
                     q_ref[below] = q_ref[below] - change[below, BLK:]
@@ -108,13 +117,12 @@
                     out_ref[0, :, there] = jnp.zeros((BLK, BLK), jnp.float32)
 
 
-def factor_rows(target_blocks, total):
-    width = target_blocks.shape[1]
+def factor_rows(updated, width):
     vmem = pl.BlockSpec(memory_space=pltpu.VMEM)
     return pl.pallas_call(
         cholesky_kernel,
         out_shape=jax.ShapeDtypeStruct((1, BLK, width), jnp.float32),
-        in_specs=[vmem, vmem],
+        in_specs=[vmem],
         out_specs=vmem,
         scratch_shapes=[
             pltpu.VMEM((width, width), jnp.float32),
@@ -123,9 +131,9 @@
         ],
         compiler_params=pltpu.CompilerParams(vmem_limit_bytes=24 * 2**20),
         name="factor",
-    )(target_blocks, total)
-
-def routed(parent, off_blocks, inv_factors, arrow_rows):
+    )(updated)
+
+def routed(parent, off_blocks, inv_factors, arrow_rows, target_blocks, arrow_block):
     supers = lax.axis_size("super")
     sources, fanout, slab_rows, block_width = off_blocks.shape
     item_count = sources * fanout
@@ -163,22 +171,24 @@
     )
     schur = lax.psum(schur_local.astype(jnp.bfloat16), "col")
     blocks = block_width // BLK
-    total = jnp.stack(
+    whole = target_blocks[0] - schur.astype(jnp.float32)
+    updated = jnp.stack(
         [
-            schur[r * BLK : (r + 1) * BLK, c * BLK : (c + 1) * BLK]
+            whole[r * BLK : (r + 1) * BLK, c * BLK : (c + 1) * BLK]
             for r, c in block_pairs(blocks)
         ]
     )
-    return total, arrow_total
+    return updated, arrow_block - arrow_total
 
 
 def exchange_kernel(
     supers, cols, fanout,
-    parent_ref, off_ref, inv_ref, arrow_rows_ref, arrow_block_ref,
-    total_ref, arrow_ref,
+    parent_ref, off_hbm, inv_ref, arrow_rows_hbm, target_hbm, arrow_block_hbm,
+    updated_ref, arrow_ref,
+    off_ref, arrow_rows_ref, target_ref, arrow_block_ref,
     inv_all, outgoing, off_all, panel, sums, landed, arrow_all, total,
     inv_send, inv_recv, off_send, off_recv, sum_send, sum_recv,
-    arrow_send, arrow_recv, cast_send, cast_recv,
+    arrow_send, arrow_recv, cast_send, cast_recv, load_sem,
 ):
     sources = inv_ref.shape[0]
     slab = inv_ref.shape[1]
@@ -193,6 +203,21 @@
     diagonal = 2 * (1 - y) + 1 - core
     peers = (beside, across, diagonal)
 
+    loads = [
+        pltpu.make_async_copy(src, dst, load_sem.at[n])
+        for n, (src, dst) in enumerate(
+            (
+                (off_hbm, off_ref),
+                (inv_ref, inv_all.at[:, me_c]),
+                (arrow_rows_hbm, arrow_rows_ref),
+                (target_hbm, target_ref),
+                (arrow_block_hbm, arrow_block_ref),
+            )
+        )
+    ]
+    for load in loads:
+        load.start()
+
     barrier = pltpu.get_barrier_semaphore()
     for peer in peers:
         pl.semaphore_signal(
@@ -242,6 +267,7 @@
             second_source = jnp.where(hit, source, second_source)
         return (first, second), (first_source, second_source)
 
+    loads[0].wait()
     off_copies = {}
     own_sources = []
     for t in range(rounds):
@@ -263,8 +289,8 @@
         own_sources.append(chosen_sources)
         for m in range(2):
             off_all[t, m, me_c] = off_ref[chosen[m]]
-    for j in range(sources):
-        inv_all[j, me_c] = inv_ref[j]
+    for load in loads[1:]:
+        load.wait()
 
     inv_across.wait_recv()
     inv_onward = remote(
@@ -300,6 +326,15 @@
         copy.start()
         arrow_copies.append(copy)
 
+    def part(r):
+        return slice(pairs.index((r, r)), pairs.index((r, blocks - 1)) + 1)
+
+    def sum_copy(t, r, slot, sup, col):
+        here = pl.ds(part(r).start, part(r).stop - part(r).start)
+        return remote(
+            sums.at[t, here], landed.at[slot, here], sum_send.at[t, r], sum_recv.at[slot, r], sup, col
+        )
+
     for t in range(rounds):
         for k in range(3):
             off_copies[k, t].wait_recv()
@@ -310,6 +345,7 @@
                 nt,
                 preferred_element_type=jnp.float32,
             ).astype(jnp.bfloat16)
+        p = parent_of(me_c, t)
         for r in range(blocks):
             product = lax.dot_general(
                 panel[r * BLK : (r + 1) * BLK, :],
@@ -319,52 +355,56 @@
             ).astype(jnp.bfloat16)
             for c in range(r, blocks):
                 sums[t, pairs.index((r, c))] = product[:, (c - r) * BLK : (c - r + 1) * BLK]
-        p = parent_of(me_c, t)
-
-        @pl.when(p != me_s)
-        def _():
-            remote(
-                sums.at[t], landed.at[me_s], sum_send.at[t], sum_recv.at[me_s], p, me_c
-            ).start()
-
-        @pl.when(p == me_s)
-        def _():
-            landed[me_s] = sums[t]
+
+            @pl.when(p != me_s)
+            def _():
+                sum_copy(t, r, me_s, p, me_c).start()
+
+            @pl.when(p == me_s)
+            def _():
+                landed[me_s, part(r)] = sums[t, part(r)]
 
     chief = lax.rem(me_s, cols)
 
-    def cast(n, col):
-        return remote(total, total, cast_send.at[n], cast_recv.at[0], me_s, col)
+    def cast(n, r, col):
+        return remote(
+            total.at[pl.ds(part(r).start, blocks - r)], total.at[pl.ds(part(r).start, blocks - r)], cast_send.at[n, r], cast_recv.at[r], me_s, col
+        )
 
     @pl.when(me_c == chief)
     def _():
-        for d in range(1, supers):
-            s = lax.rem(me_s + d, supers)
-            remote(
-                sums.at[0], landed.at[s], sum_send.at[0], sum_recv.at[s], me_s, beside
-            ).wait_recv()
-        for b in range(len(pairs)):
-            acc = landed[0, b].astype(jnp.float32)
-            for s in range(1, supers):
-                acc = acc + landed[s, b].astype(jnp.float32)
-            total[b] = acc.astype(jnp.bfloat16)
-        first, second = cast(0, across), cast(1, beside)
-        first.start()
-        second.start()
-        first.wait_send()
-        second.wait_send()
+        for r in range(blocks):
+            for d in range(1, supers):
+                sum_copy(0, r, lax.rem(me_s + d, supers), me_s, beside).wait_recv()
+            for b in range(part(r).start, part(r).stop):
+                acc = landed[0, b].astype(jnp.float32)
+                for s in range(1, supers):
+                    acc = acc + landed[s, b].astype(jnp.float32)
+                total[b] = acc.astype(jnp.bfloat16)
+            cast(0, r, across).start()
+            cast(1, r, beside).start()
+        for r in range(blocks):
+            cast(0, r, across).wait_send()
+            cast(1, r, beside).wait_send()
 
     @pl.when(me_c != chief)
     def _():
-        cast(0, beside).wait_recv()
+        for r in range(blocks):
+            cast(0, r, beside).wait_recv()
+
+            @pl.when(across == chief)
+            def _():
+                cast(1, r, beside).start()
 
     @pl.when(across == chief)
     def _():
-        onward = cast(1, beside)
-        onward.start()
-        onward.wait_send()
-
-    total_ref[...] = total[...]
+        for r in range(blocks):
+            cast(1, r, beside).wait_send()
+
+    for n, (r, c) in enumerate(pairs):
+        updated_ref[n] = target_ref[
+            0, r * BLK : (r + 1) * BLK, c * BLK : (c + 1) * BLK
+        ] - total[n].astype(jnp.float32)
 
     for copy in arrow_copies:
         copy.wait_recv()
@@ -380,29 +420,33 @@
 
         @pl.when(p != me_s)
         def _():
-            remote(
-                sums.at[t], landed.at[me_s], sum_send.at[t], sum_recv.at[me_s], p, me_c
-            ).wait_send()
-
-
-def exchanged(parent, off_blocks, inv_factors, arrow_rows, arrow_block):
+            for r in range(blocks):
+                sum_copy(t, r, me_s, p, me_c).wait_send()
+
+
+def exchanged(parent, off_blocks, inv_factors, arrow_rows, target_blocks, arrow_block):
     supers, cols = lax.axis_size("super"), lax.axis_size("col")
     sources, fanout, slab, width = off_blocks.shape
     arrow = arrow_block.shape[0]
     rounds = supers // cols
     count = len(block_pairs(width // BLK))
     vmem = pl.BlockSpec(memory_space=pltpu.VMEM)
+    hbm = pl.BlockSpec(memory_space=pltpu.HBM)
     bf16, f32 = jnp.bfloat16, jnp.float32
     dma = pltpu.SemaphoreType.DMA
     return pl.pallas_call(
         functools.partial(exchange_kernel, supers, cols, fanout),
         out_shape=(
-            jax.ShapeDtypeStruct((count, BLK, BLK), bf16),
+            jax.ShapeDtypeStruct((count, BLK, BLK), f32),
             jax.ShapeDtypeStruct((arrow, arrow), f32),
         ),
-        in_specs=[pl.BlockSpec(memory_space=pltpu.SMEM)] + [vmem] * 4,
+        in_specs=[pl.BlockSpec(memory_space=pltpu.SMEM)] + [hbm] * 5,
         out_specs=(vmem, vmem),
         scratch_shapes=[
+            pltpu.VMEM((sources * fanout, slab, width), bf16),
+            pltpu.VMEM((sources, arrow, width), bf16),
+            pltpu.VMEM((1, width, width), f32),
+            pltpu.VMEM((arrow, arrow), f32),
             pltpu.VMEM((sources, cols, slab, width), bf16),
             pltpu.VMEM((cols - 1, rounds, 2, slab, width), bf16),
             pltpu.VMEM((rounds, 2, cols, slab, width), bf16),
@@ -415,29 +459,36 @@
             dma((3,)),
             dma((3, rounds)),
             dma((3, rounds)),
-            dma((rounds,)),
+            dma((rounds, width // BLK)),
+            dma((supers, width // BLK)),
             dma((supers,)),
             dma((supers,)),
-            dma((supers,)),
-            dma((2,)),
-            dma((1,)),
+            dma((2, width // BLK)),
+            dma((width // BLK,)),
+            dma((5,)),
         ],
         compiler_params=pltpu.CompilerParams(
             collective_id=0, has_side_effects=True, vmem_limit_bytes=40 * 2**20
         ),
         name="exchange",
-    )(parent, off_blocks.reshape(sources * fanout, slab, width), inv_factors, arrow_rows, arrow_block)
+    )(
+        parent,
+        off_blocks.reshape(sources * fanout, slab, width),
+        inv_factors,
+        arrow_rows,
+        target_blocks,
+        arrow_block,
+    )
 
 
 def shards(parent, off_blocks, inv_factors, arrow_rows, target_blocks, arrow_block):
     supers, cols = lax.axis_size("super"), lax.axis_size("col")
     entries = off_blocks.shape[0] * off_blocks.shape[1]
-    if cols == 4 and supers == 2 * cols and entries == 2 * supers:
-        total, arrow_update = exchanged(parent, off_blocks, inv_factors, arrow_rows, arrow_block)
-    else:
-        total, arrow_total = routed(parent, off_blocks, inv_factors, arrow_rows)
-        arrow_update = arrow_block - arrow_total
-    return factor_rows(target_blocks, total), arrow_update
+    form = exchanged if cols == 4 and supers == 2 * cols and entries == 2 * supers else routed
+    updated, arrow_update = form(
+        parent, off_blocks, inv_factors, arrow_rows, target_blocks, arrow_block
+    )
+    return factor_rows(updated, target_blocks.shape[1]), arrow_update
 
 
 def solution(mesh):

time: 104 us -> 82 us (0.79)
  Pallas kernels: 95.7 us -> 73.3 us
  local copies, waits for them, and re-layouts: 5.63 us -> 6.85 us
    pallas_call x1, Pallas kernels: 35.7 us -> 16.4 us  [factor_rows(): pl.pallas_call(cholesky_kernel, out_shape=jax.ShapeDtypeStruct((1, BLK, w...]
    pallas_call x1, Pallas kernels: 59.9 us -> 56.9 us  [exchanged(): pl.pallas_call(functools.partial(exchange_kernel, supers, cols, fanout),...]
    unnamed x13, local copies, waits for them, and re-layouts: 5.63 us -> 6.85 us
where the time goes in v3:
time: 82 us; the launch traced here: 80.8 us
  Pallas kernels  73.3 us (89%)
  local copies, waits for them, and re-layouts  6.85 us (8%)
    pallas_call x1, Pallas kernels, exchanged(): pl.pallas_call(functools.partial(exchange_kernel, supers, cols, fanout),...  56.9 us
    pallas_call x1, Pallas kernels, factor_rows(): pl.pallas_call(cholesky_kernel, out_shape=jax.ShapeDtypeStruct((1, BLK, w...  16.4 us
    unnamed x13, local copies, waits for them, and re-layouts  6.85 us

profile of v3, /device:TPU:0, one launch (start us, length us, event | category | flops | bytes accessed | tf_op | source)
XLA Modules:
  0.0 80.8 jit_solution(18388931888986468803)
XLA Ops:
  0.6 0.0 copy-start
  0.6 1.6 %copy-done = bf16[4,4,128,512]{3,2,1,0:T(8,128)(2,1)S(1)} copy-done((bf16[4,4,128,512]{3,2,1,0:T(8,128)(2,1)S(1)}, bf16[4,4,128,512]{3,2,1,0:T(8,128)(2,1)}, u32[]{:S(2)}) %copy-start) | copy-done | bytes 2097176
  2.2 0.0 copy-start.1
  2.2 1.2 %copy-done.1 = f32[1,512,512]{2,1,0:T(8,128)S(1)} copy-done((f32[1,512,512]{2,1,0:T(8,128)S(1)}, f32[1,512,512]{2,1,0:T(8,128)}, u32[]{:S(2)}) %copy-start.1) | copy-done | bytes 1048600
  3.4 0.0 copy-start.2
  3.5 1.0 %copy-done.2 = bf16[4,128,512]{2,1,0:T(8,128)(2,1)S(1)} copy-done((bf16[4,128,512]{2,1,0:T(8,128)(2,1)S(1)}, bf16[4,128,512]{2,1,0:T(8,128)(2,1)}, u32[]{:S(2)}) %copy-start.2) | copy-done | bytes 524312
  4.5 0.0 copy-start.3
  4.5 0.9 %copy-done.3 = bf16[4,64,512]{2,1,0:T(8,128)(2,1)S(1)} copy-done((bf16[4,64,512]{2,1,0:T(8,128)(2,1)S(1)}, bf16[4,64,512]{2,1,0:T(8,128)(2,1)}, u32[]{:S(2)}) %copy-start.3) | copy-done | bytes 262168
  5.4 0.0 copy-start.4
  5.4 0.8 copy-done.4
  6.2 0.0 copy-start.5
  6.2 0.7 copy-done.5
  6.9 56.9 %exchange.1 = (f32[10,128,128]{2,1,0:T(8,128)S(1)}, f32[64,64]{1,0:T(8,128)S(1)}) custom-call(s32[4,4]{1,0:T(4,128)S(1)} %copy-done.5, bf16[16,128,512]{2,1,0:T(8,128)(2,1)S(1)} %bitcast.1, bf16[4,128,512]{2,1,0:T(8,128)(2,1)S(1)} %copy-done.2, bf16[4,64,512]{2,1,0:T(8,128)(2,1)S(1)} %copy-done.3, f32[1,512,512]{2,1,0:T(8,128)S(1)} %copy-done.1, ...), custom_call_target="tpu_custom_call" | custom-call | tf_op jit(solution)/shard_map/exchange/pallas_call | solution.py:437
  63.8 16.4 %factor.1 = f32[1,128,512]{2,1,0:T(8,128)} custom-call(f32[10,128,128]{2,1,0:T(8,128)S(1)} %get-tuple-element.4.updated_ref), custom_call_target="tpu_custom_call" | custom-call | tf_op jit(solution)/shard_map/factor/pallas_call | solution.py:122
  80.2 0.6 copy.9
Async XLA Ops:
  0.6 1.6 %copy-start = (bf16[4,4,128,512]{3,2,1,0:T(8,128)(2,1)S(1)}, bf16[4,4,128,512]{3,2,1,0:T(8,128)(2,1)}, u32[]{:S(2)}) copy-start(bf16[4,4,128,512]{3,2,1,0:T(8,128)(2,1)} %param.7) | copy-start | bytes 6291460
  2.2 1.2 %copy-start.1 = (f32[1,512,512]{2,1,0:T(8,128)S(1)}, f32[1,512,512]{2,1,0:T(8,128)}, u32[]{:S(2)}) copy-start(f32[1,512,512]{2,1,0:T(8,128)} %target_hbm.1) | copy-start | bytes 3145732
  3.4 1.0 %copy-start.2 = (bf16[4,128,512]{2,1,0:T(8,128)(2,1)S(1)}, bf16[4,128,512]{2,1,0:T(8,128)(2,1)}, u32[]{:S(2)}) copy-start(bf16[4,128,512]{2,1,0:T(8,128)(2,1)} %inv_ref.1) | copy-start | bytes 1572868
  4.5 0.9 %copy-start.3 = (bf16[4,64,512]{2,1,0:T(8,128)(2,1)S(1)}, bf16[4,64,512]{2,1,0:T(8,128)(2,1)}, u32[]{:S(2)}) copy-start(bf16[4,64,512]{2,1,0:T(8,128)(2,1)} %arrow_rows_hbm.1) | copy-start | bytes 786436
  5.4 0.8 copy-start.4
  6.2 0.7 copy-start.5

commit v4 on v3

--- a/solution.py
+++ b/solution.py
@@ -468,7 +468,7 @@
             dma((5,)),
         ],
         compiler_params=pltpu.CompilerParams(
-            collective_id=0, has_side_effects=True, vmem_limit_bytes=40 * 2**20
+            collective_id=0, has_side_effects=True, vmem_limit_bytes=65408 * 2**10
         ),
         name="exchange",
     )(

time: 82 us -> 78.4 us (0.956)
  local copies, waits for them, and re-layouts: 6.85 us -> 2.45 us
  Pallas kernels: 73.3 us -> 74.2 us
    unnamed x13 -> x3, local copies, waits for them, and re-layouts: 6.85 us -> 2.45 us
    pallas_call x1, Pallas kernels: 56.9 us -> 57.8 us  [exchanged(): pl.pallas_call(functools.partial(exchange_kernel, supers, cols, fanout),...]
where the time goes in v4:
time: 78.4 us; the launch traced here: 77.3 us
  Pallas kernels  74.2 us (95%)
  local copies, waits for them, and re-layouts  2.45 us (3%)
    pallas_call x1, Pallas kernels, exchanged(): pl.pallas_call(functools.partial(exchange_kernel, supers, cols, fanout),...  57.8 us
    pallas_call x1, Pallas kernels, factor_rows(): pl.pallas_call(cholesky_kernel, out_shape=jax.ShapeDtypeStruct((1, BLK, w...  16.4 us
    unnamed x3, local copies, waits for them, and re-layouts  2.45 us

profile of v4, /device:TPU:0, one launch (start us, length us, event | category | flops | bytes accessed | tf_op | source)
XLA Modules:
  0.0 77.3 jit_solution(11073274707199092160)
XLA Ops:
  0.6 57.8 %exchange.1 = (f32[10,128,128]{2,1,0:T(8,128)}, f32[64,64]{1,0:T(8,128)}) custom-call(s32[4,4]{1,0:T(4,128)} %parent_ref.1, bf16[16,128,512]{2,1,0:T(8,128)(2,1)} %bitcast.1, bf16[4,128,512]{2,1,0:T(8,128)(2,1)} %inv_ref.1, bf16[4,64,512]{2,1,0:T(8,128)(2,1)} %arrow_rows_hbm.1, f32[1,512,512]{2,1,0:T(8,128)} %target_hbm.1, f32[64,64]{1,0:T(8,128)} %arrow_block_hbm.1), custom_call_target="tpu_custom_call" | custom-call | tf_op jit(solution)/shard_map/exchange/pallas_call | solution.py:437
  58.5 0.0 copy-start
  58.5 1.1 %copy-done = f32[10,128,128]{2,1,0:T(8,128)S(1)} copy-done((f32[10,128,128]{2,1,0:T(8,128)S(1)}, f32[10,128,128]{2,1,0:T(8,128)}, u32[]{:S(2)}) %copy-start) | copy-done | bytes 655384
  59.6 16.4 %factor.1 = f32[1,128,512]{2,1,0:T(8,128)} custom-call(f32[10,128,128]{2,1,0:T(8,128)S(1)} %copy-done), custom_call_target="tpu_custom_call" | custom-call | tf_op jit(solution)/shard_map/factor/pallas_call | solution.py:122
  75.9 1.4 %copy.9 = f32[64,64]{1,0:T(8,128)} copy(f32[64,64]{1,0:T(8,128)} %get-tuple-element.9) | data formatting | bytes 32768
Async XLA Ops:
  58.5 1.1 %copy-start = (f32[10,128,128]{2,1,0:T(8,128)S(1)}, f32[10,128,128]{2,1,0:T(8,128)}, u32[]{:S(2)}) copy-start(f32[10,128,128]{2,1,0:T(8,128)} %get-tuple-element.4.updated_ref) | copy-start | bytes 1966084
